TPU v7x, 512 devices: a whole 4x8x8 slice. The times are simulated.
512 devices in a mesh: group: 16 (over y, core), member: 32 (over z, x).
Axes of the slice: x: 4, y: 8, z: 8, core: 2. Of those that a mesh axis runs over, the one named last changes fastest.
Arguments:
- cache: bfloat16 [2048, 512, 576], P(('group', 'member')), may hold values from -8 to 8
- cache_len: int32 [2048], P(('group', 'member')), may hold values from 1 to 512, as said below
- query: bfloat16 [2048, 2, 128, 576], P(('group', 'member')), may hold values from -32 to 32
- fresh: bfloat16 [65536, 576], P(('group', 'member')), may hold values from -4 to 4
- fresh_dest: int32 [65536, 1], P(('group', 'member')), may hold values from 0 to 15; in each aligned block of 128 rows (0 to 127, 128 to 255, ...) at most 16 rows name the same one
- fresh_slot: int32 [65536], P(('group', 'member')), may hold values from 0 to 3
- token_group: int32 [4096, 1], P('group'), may hold values from 0 to 15; in each aligned block of 256 rows (0 to 255, 256 to 511, ...) at most 32 rows name the same one
- w_uv: bfloat16 [128, 512, 128], P('member'), may hold values from -0.25 to 0.25
Outputs:
- dispatched: bfloat16 [8192, 16384], P('group', 'member')
Inputs may be any that keep to these rules, and one draw needn't show every extreme that they name: `cache_len`: every request has at least one valid resident row, and some request has 512 in every draw. `fresh_dest`: of the 128 rows of one device, at most 16 name the same group; some group is named by exactly 16 rows. `token_group`: of the 256 tokens of one group, at most 32 name the same expert group; some expert group is named by exactly 32.
All inputs are finite; a program needn't handle non-finite values.
Results may differ from a plain program's by a relative error of at most 0.0057.
Values may be sent and summed in bfloat16 or wider, within the bound.
A program may use at most 64 MiB of HBM per device.

v0:
```python
import jax
import jax.numpy as jnp
from jax import lax
from jax.sharding import PartitionSpec as P

KVL = 512
ROPE = 64
NOPE = 128


def place_rows(targets, peers, cap):
    onehot = (targets[:, None] == jnp.arange(peers, dtype=jnp.int32)[None, :]).astype(jnp.int32)
    before = jnp.sum(jnp.cumsum(onehot, 0) * onehot, 1) - 1
    return targets * cap + before


def attend(query, cache, lengths, arrived, labels):
    count = cache.shape[0]
    scale = (NOPE + ROPE) ** (-0.5)
    near = jnp.einsum("bqhw,blw->bqhl", query, cache, preferred_element_type=jnp.float32) * scale
    far = jnp.einsum("bqhw,aw->bqha", query, arrived, preferred_element_type=jnp.float32) * scale
    near_mask = (jnp.arange(cache.shape[1], dtype=jnp.int32)[None, :] < lengths[:, None])[
        :, None, None, :
    ]
    far_mask = (labels[None, :] == jnp.arange(count, dtype=jnp.int32)[:, None])[:, None, None, :]
    near = jnp.where(near_mask, near, -jnp.inf)
    far = jnp.where(far_mask, far, -jnp.inf)
    top = jnp.maximum(jnp.max(near, -1, keepdims=True), jnp.max(far, -1, keepdims=True))
    near_p = jnp.exp(near - top)
    far_p = jnp.exp(far - top)
    total = jnp.sum(near_p, -1, keepdims=True) + jnp.sum(far_p, -1, keepdims=True)
    near_w = (near_p / total).astype(jnp.bfloat16)
    far_w = (far_p / total).astype(jnp.bfloat16)
    latent = jnp.einsum(
        "bqhl,blc->bqhc", near_w, cache[..., :KVL], preferred_element_type=jnp.float32
    )
    latent = latent + jnp.einsum(
        "bqha,ac->bqhc", far_w, arrived[:, :KVL], preferred_element_type=jnp.float32
    )
    return latent.astype(jnp.bfloat16)


def local(cache, cache_len, query, fresh, fresh_dest, fresh_slot, token_group, w_uv):
    groups = lax.axis_size("group")
    count = cache.shape[0]
    dest = fresh_dest[:, 0]
    codes = (dest * count + fresh_slot).astype(jnp.bfloat16)
    arrived, every_code = (
        lax.all_gather(fresh, "group", axis=0, tiled=True),
        lax.all_gather(codes, "group", axis=0, tiled=True),
    )
    mine = lax.axis_index("group")
    whole = every_code.astype(jnp.int32)
    labels = jnp.where(whole // count == mine, whole - mine * count, -1)
    latent = attend(query, cache, cache_len, arrived, labels)
    lifted = jnp.einsum(
        "bqhc,hcv->bqhv",
        lax.all_to_all(latent, "member", split_axis=2, concat_axis=0, tiled=True),
        w_uv,
        preferred_element_type=jnp.float32,
    ).astype(jnp.bfloat16)
    tok_rows = lifted.shape[0] * lifted.shape[1]
    values = lifted.reshape(tok_rows, lifted.shape[2] * lifted.shape[3])
    cape = 2 * tok_rows // groups
    where_tok = place_rows(token_group[:, 0], groups, cape)
    packed = jnp.zeros((groups * cape, values.shape[1]), jnp.bfloat16).at[where_tok].set(values)
    received = lax.all_to_all(
        packed.reshape(groups, cape, values.shape[1]),
        "group",
        split_axis=0,
        concat_axis=0,
        tiled=True,
    )
    return received.reshape(groups * cape, values.shape[1])


def solution(mesh):
    placed = (
        P(("group", "member"), None, None),
        P(("group", "member")),
        P(("group", "member"), None, None, None),
        P(("group", "member"), None),
        P(("group", "member"), None),
        P(("group", "member")),
        P("group", None),
        P("member", None, None),
    )
    return jax.shard_map(
        local, mesh=mesh, in_specs=placed, out_specs=P("group", "member"), check_vma=False
    )
```

profile of v0, /device:TPU:1, one launch (start us, length us, event | category | flops | bytes accessed | tf_op | source)
XLA Modules:
  0.0 146.6 jit_solution(3691275840237997921)
XLA Ops:
  6.5 0.7 all-gather.3.cloned.1.call-update
  7.3 0.7 fusion.30
  7.9 20.7 %all-gather = bf16[16,1,128]{2,1,0:T(2,128)(2,1)S(1)} all-gather(bf16[1,1,128]{2,1,0:T(2,128)(2,1)S(1)} %fusion.30), channel_id=1, replica_groups=mesh['group'=16,'member'=32] {'group'}, dimensions={0}, use_global_device_ids=true | all-gather | bytes 4352 | tf_op jit(solution)/shard_map/all_gather | solution.py:50
  28.7 0.7 iota_compare_fusion.3
  29.4 2.8 %fusion.10 = (f32[4,2,128]{2,1,0:T(2,128)S(1)}, f32[4,2,128,512]{3,2,1,0:T(8,128)S(1)}) fusion(pred[4,512]{1,0:T(4,128)(4,1)S(1)} %iota_compare_fusion.3, bf16[4,2,128,576]{2,3,1,0:T(8,128)(2,1)S(1)} %copy-done, bf16[4,512,576]{1,2,0:T(8,128)(2,1)} %param.8), kind=kOutput, calls=%fused_computation.19 | convolution fusion | flops 605551616 | bytes 5642240 | tf_op jit(solution)/shard_map/bqhw,blw->bqhl/dot_general | solution.py:20
  32.2 27.5 %all-gather.3.cloned.1.call-done = bf16[2048,576]{0,1:T(8,128)(2,1)} async-done(((bf16[128,576]{0,1:T(8,128)(2,1)}), bf16[2048,576]{0,1:T(8,128)(2,1)}) %all-gather.3.cloned.1.call-update) | async-done | bytes 2359312 | tf_op jit(solution)/shard_map/all_gather | solution.py:49
  59.7 5.6 %fusion = (f32[4,2,128]{2,1,0:T(2,128)S(1)}, f32[4,2,128,2048]{3,2,1,0:T(8,128)S(1)}) fusion(pred[4,2048]{1,0:T(4,128)(4,1)S(1)} %iota_compare_fusion, bf16[4,2,128,576]{2,3,1,0:T(8,128)(2,1)S(1)} %copy-done, bf16[2048,576]{0,1:T(8,128)(2,1)} %all-gather.3.cloned.1.call-done), kind=kOutput, calls=%fused_computation.4 | convolution fusion | flops 2422209536 | bytes 11939840 | tf_op jit(solution)/shard_map/bqhw,aw->bqha/dot_general | solution.py:21
  65.3 1.9 %fusion.1 = f32[4,2,128]{2,1,0:T(2,128)S(1)} fusion(f32[4,2,128,2048]{3,2,1,0:T(8,128)S(1)} %get-tuple-element.8, f32[4,2,128]{2,1,0:T(2,128)S(1)} %max.8, pred[4,2048]{1,0:T(4,128)(4,1)S(1)} %iota_compare_fusion), kind=kLoop, calls=%fused_computation.5 | loop fusion | flops 8387584 | bytes 8404992 | tf_op jit(solution)/shard_map/reduce_sum | solution.py:31
  67.2 0.6 fusion.11
  67.9 1.1 fusion.7
  69.0 0.6 copy-done.1
  69.5 2.6 %add_convert_fusion = bf16[4,2,128,512]{3,2,1,0:T(8,128)(2,1)S(1)} fusion(f32[4,2,128,512]{3,2,1,0:T(8,128)S(1)} %fusion.7, bf16[2048,576]{0,1:T(8,128)(2,1)S(1)} %copy-done.1, f32[4,2,128,2048]{3,2,1,0:T(8,128)S(1)} %get-tuple-element.8, f32[4,2,128]{2,1,0:T(2,128)S(1)} %add.39, f32[4,2,128]{2,1,0:T(2,128)S(1)} %max.8, ...), kind=kOutput, calls=%fused_computation.14 | convolution fusion | flops 2159017984 | bytes 13647872 | tf_op jit(solution)/shard_map/bqha,ac->bqhc/dot_general | solution.py:37
  72.1 2.1 %copy.20 = bf16[4,2,128,512]{3,1,0,2:T(2,128)(2,1)} copy(bf16[4,2,128,512]{3,2,1,0:T(8,128)(2,1)S(1)} %add_convert_fusion) | data formatting | bytes 2097152 | tf_op jit(solution)/shard_map/convert_element_type | solution.py:40
  74.2 10.1 %all-to-all-start = ((bf16[4,2,128,512]{3,1,0,2:T(2,128)(2,1)}), bf16[4,2,128,512]{3,1,0,2:T(2,128)(2,1)S(1)}, u32[]{:S(2)}, u32[]{:S(2)}) async-start(bf16[4,2,128,512]{3,1,0,2:T(2,128)(2,1)} %copy.20), calls=%async_computation | async-start | bytes 2097152 | tf_op jit(solution)/shard_map/all_to_all | solution.py:58
  84.3 0.6 reduce-window.6
  84.9 0.2 slice_reduce_fusion
  85.2 25.8 %all-to-all-done = bf16[4,2,128,512]{3,1,0,2:T(2,128)(2,1)S(1)} async-done(((bf16[4,2,128,512]{3,1,0,2:T(2,128)(2,1)}), bf16[4,2,128,512]{3,1,0,2:T(2,128)(2,1)S(1)}, u32[]{:S(2)}, u32[]{:S(2)}) %all-to-all-start) | async-done | bytes 1048608 | tf_op jit(solution)/shard_map/all_to_all | solution.py:58
  111.0 0.4 copy.38
  111.4 0.3 all_to_all.19
  111.7 1.5 fusion.12
  113.2 0.2 copy.22
  113.4 1.7 %scatter_custom_fusion = bf16[512,512]{1,0:T(8,128)(2,1)S(1)} fusion(s32[256]{0:T(256)S(1)} %bitcast.85, bf16[32,8,4,128]{3,2,1,0:T(4,128)(2,1)S(1)} %bitcast.80, bf16[]{:T(256)} %constant.14.clone.1), kind=kCustom, calls=%fused_computation.30 | custom fusion | bytes 786434 | tf_op jit(solution)/shard_map/scatter | solution.py:66
  115.1 23.9 %all_to_all.23 = bf16[16,32,512]{2,1,0:T(8,128)(2,1)S(1)} all-to-all(bf16[16,32,512]{2,1,0:T(8,128)(2,1)S(1)} %bitcast.78), channel_id=1, replica_groups=mesh['group'=16,'member'=32] {'group'}, dimensions={0} | all-to-all | bytes 1048576 | tf_op jit(solution)/shard_map/all_to_all | solution.py:67
  139.0 0.8 copy.40
  (19 shorter events, 0.2 us)
Async XLA Ops:
  6.5 22.9 %copy-start = (bf16[4,2,128,576]{2,3,1,0:T(8,128)(2,1)S(1)}, bf16[4,2,128,576]{2,3,1,0:T(8,128)(2,1)}, u32[]{:S(2)}) copy-start(bf16[4,2,128,576]{2,3,1,0:T(8,128)(2,1)} %param.10) | copy-start | bytes 3538948
  6.5 53.2 %all-gather.3.cloned.1.call-start = ((), (), s32[]{:S(2)}) async-start(), calls=%async_computation.2 | async-start | bytes 2506752 | tf_op jit(solution)/shard_map/all_gather | solution.py:49
  65.3 2.5 %copy-start.3 = (bf16[4,512,576]{1,2,0:T(8,128)(2,1)S(1)}, bf16[4,512,576]{1,2,0:T(8,128)(2,1)}, u32[]{:S(2)}) copy-start(bf16[4,512,576]{1,2,0:T(8,128)(2,1)} %param.8) | copy-start | bytes 7077892
  67.9 1.7 %copy-start.1 = (bf16[2048,576]{0,1:T(8,128)(2,1)S(1)}, bf16[2048,576]{0,1:T(8,128)(2,1)}, u32[]{:S(2)}) copy-start(bf16[2048,576]{0,1:T(8,128)(2,1)} %all-gather.3.cloned.1.call-done) | copy-start | bytes 7077892
  72.1 12.2 %copy-start.2 = (s32[256,1]{0,1:T(1,128)S(1)}, s32[256,1]{0,1:T(1,128)}, u32[]{:S(2)}) copy-start(s32[256,1]{0,1:T(1,128)} %param.14) | copy-start | bytes 3076
  74.2 36.8 %all-to-all-start = ((bf16[4,2,128,512]{3,1,0,2:T(2,128)(2,1)}), bf16[4,2,128,512]{3,1,0,2:T(2,128)(2,1)S(1)}, u32[]{:S(2)}, u32[]{:S(2)}) async-start(bf16[4,2,128,512]{3,1,0,2:T(2,128)(2,1)} %copy.20), calls=%async_computation | async-start | bytes 2097152 | tf_op jit(solution)/shard_map/all_to_all | solution.py:58
Sparse Core Ops, SparseCore 0:
  9.4 50.2 all-gather.2
where the time goes:
time: 147 us
  waiting for transfers between devices  54 us (37%)
  blocking collectives  44.6 us (30%)
  matrix products  13.5 us (9%)
  between operations  13.5 us (9%)
  starting transfers between devices  10.1 us (7%)
  local copies, waits for them, and re-layouts  6.19 us (4%)
  other arithmetic  4.71 us (3%)
    all_gather x1, waiting for transfers between devices, local(): lax.all_gather(fresh, 'group', axis=0, tiled=True)  27.5 us
    all_to_all x1, waiting for transfers between devices, local(): lax.all_to_all(latent, 'member', split_axis=2, concat_axis=0, tiled=True)  25.8 us
    all_to_all x1, blocking collectives, local(): lax.all_to_all(packed.reshape(groups, cape, values.shape[1]), 'group', sp...  23.9 us
    all_gather x1, blocking collectives, local(): lax.all_gather(codes, 'group', axis=0, tiled=True)  20.7 us
    all_to_all x1, starting transfers between devices, local(): lax.all_to_all(latent, 'member', split_axis=2, concat_axis=0, tiled=True)  10.1 us
    dot_general x1, matrix products, attend(): jnp.einsum('bqhw,aw->bqha', query, arrived, preferred_element_type=jnp.fl...  5.58 us
  transfers between devices with their start and end apart: 2, of which 2 were waited for; matrix products, arithmetic and copies ran while one was open for 4% of the time, Pallas kernels for 0%

commit v1 on v0

--- a/solution.py
+++ b/solution.py
@@ -44,14 +44,18 @@
     groups = lax.axis_size("group")
     count = cache.shape[0]
     dest = fresh_dest[:, 0]
-    codes = (dest * count + fresh_slot).astype(jnp.bfloat16)
-    arrived, every_code = (
-        lax.all_gather(fresh, "group", axis=0, tiled=True),
-        lax.all_gather(codes, "group", axis=0, tiled=True),
-    )
-    mine = lax.axis_index("group")
-    whole = every_code.astype(jnp.int32)
-    labels = jnp.where(whole // count == mine, whole - mine * count, -1)
+    cap = 2 * fresh.shape[0] // groups
+    where_to = place_rows(dest, groups, cap)
+    marks = (fresh_slot[:, None] == jnp.arange(count, dtype=jnp.int32)[None, :]).astype(fresh.dtype)
+    rows = jnp.concatenate([fresh, marks, jnp.zeros((fresh.shape[0], ROPE - count), fresh.dtype)], 1)
+    picks = (where_to[None, :] == jnp.arange(groups * cap, dtype=jnp.int32)[:, None]).astype(fresh.dtype)
+    packed_rows = jnp.dot(picks, rows, preferred_element_type=jnp.float32).astype(fresh.dtype)
+    landed = lax.all_to_all(
+        packed_rows.reshape(groups, cap, rows.shape[1]), "group", split_axis=0, concat_axis=0, tiled=True
+    ).reshape(groups * cap, rows.shape[1])
+    arrived = landed[:, : fresh.shape[1]]
+    owned = landed[:, fresh.shape[1] : fresh.shape[1] + count]
+    labels = jnp.sum(owned * jnp.arange(1, count + 1, dtype=owned.dtype)[None, :], 1).astype(jnp.int32) - 1
     latent = attend(query, cache, cache_len, arrived, labels)
     lifted = jnp.einsum(
         "bqhc,hcv->bqhv",

time: 147 us -> 103 us (0.70)
  blocking collectives: 44.6 us -> 21.2 us
  waiting for transfers between devices: 54 us -> 36.1 us
  between operations: 13.5 us -> 0.16 us
  starting transfers between devices: 10.1 us -> 21.5 us
  matrix products: 13.5 us -> 10.3 us
  other arithmetic: 4.71 us -> 6.45 us
    all_gather x1 -> x0, waiting for transfers between devices: 27.5 us -> none  [local(): lax.all_gather(fresh, 'group', axis=0, tiled=True)]
    all_gather x1 -> x0, blocking collectives: 20.7 us -> none  [local(): lax.all_gather(codes, 'group', axis=0, tiled=True)]
    all_to_all x0 -> x1, starting transfers between devices: none -> 10.8 us  [local(): lax.all_to_all(packed_rows.reshape(groups, cap, rows.shape[1]), 'group',...]
    all_to_all x0 -> x1, waiting for transfers between devices: none -> 9.62 us  [local(): lax.all_to_all(packed_rows.reshape(groups, cap, rows.shape[1]), 'group',...]
    dot_general x1, matrix products: 5.58 us -> 1.57 us  [attend(): jnp.einsum('bqhw,aw->bqha', query, arrived, preferred_element_type=jnp.fl...]
    all_to_all x1, blocking collectives: 23.9 us -> 21.2 us  [local(): lax.all_to_all(packed.reshape(groups, cape, values.shape[1]), 'group', sp...]
    dot_general x0 -> x1, matrix products: none -> 1.99 us  [local(): jnp.dot(picks, rows, preferred_element_type=jnp.float32).astype(fresh.dtype)]
    reduce_sum x1, other arithmetic: 1.89 us -> 0.16 us  [attend(): jnp.sum(far_p, -1, keepdims=True)]
where the time goes in v1:
time: 103 us; the launch traced here: 102 us
  waiting for transfers between devices  36.1 us (35%)
  starting transfers between devices  21.5 us (21%)
  blocking collectives  21.2 us (21%)
  matrix products  10.3 us (10%)
  local copies, waits for them, and re-layouts  6.55 us (6%)
  other arithmetic  6.45 us (6%)
    all_to_all x1, waiting for transfers between devices, local(): lax.all_to_all(latent, 'member', split_axis=2, concat_axis=0, tiled=True)  26.5 us
    all_to_all x1, blocking collectives, local(): lax.all_to_all(packed.reshape(groups, cape, values.shape[1]), 'group', sp...  21.2 us
    all_to_all x1, starting transfers between devices, local(): lax.all_to_all(packed_rows.reshape(groups, cap, rows.shape[1]), 'group',...  10.8 us
    all_to_all x1, starting transfers between devices, local(): lax.all_to_all(latent, 'member', split_axis=2, concat_axis=0, tiled=True)  10.7 us
    all_to_all x1, waiting for transfers between devices, local(): lax.all_to_all(packed_rows.reshape(groups, cap, rows.shape[1]), 'group',...  9.62 us
    dot_general x1, matrix products, attend(): jnp.einsum('bqhw,blw->bqhl', query, cache, preferred_element_type=jnp.flo...  2.79 us
    convert_element_type x1, local copies, waits for them, and re-layouts, attend(): return latent.astype(jnp.bfloat16)  2.07 us
  transfers between devices with their start and end apart: 2, of which 2 were waited for; matrix products, arithmetic and copies ran while one was open for 4% of the time, Pallas kernels for 0%

profile of v1, /device:TPU:1, one launch (start us, length us, event | category | flops | bytes accessed | tf_op | source)
XLA Modules:
  0.0 102.3 jit_solution(6313941828258376452)
XLA Ops:
  0.0 0.8 fusion.30
  1.0 0.8 select_reduce_fusion
  1.8 0.7 add_add_fusion
  2.5 0.7 fusion.34
  3.3 2.0 %convolution_convert_fusion = bf16[256,640]{1,0:T(8,128)(2,1)} fusion(bf16[128,4]{0,1:T(4,128)(2,1)S(1)} %fusion.34, bf16[128,576]{0,1:T(8,128)(2,1)} %param.11, bf16[640]{0:T(1024)(128)(2,1)S(1)} %pad.2.clone, s32[128]{0:T(128)S(1)} %add_add_fusion), kind=kOutput, calls=%fused_computation.15 | convolution fusion | flops 42631168 | bytes 477952 | tf_op jit(solution)/shard_map/dot_general | solution.py:52
  5.2 10.8 %all-to-all-start = ((bf16[16,16,640]{2,1,0:T(8,128)(2,1)}), bf16[16,16,640]{2,1,0:T(8,128)(2,1)}, u32[]{:S(2)}, u32[]{:S(2)}) async-start(bf16[16,16,640]{2,1,0:T(8,128)(2,1)} %bitcast.8), calls=%async_computation | async-start | bytes 655360 | tf_op jit(solution)/shard_map/all_to_all | solution.py:53
  16.1 0.7 iota_compare_fusion.5
  16.8 2.8 %fusion.5 = (f32[4,2,128]{2,1,0:T(2,128)S(1)}, f32[4,2,128,512]{3,2,1,0:T(8,128)S(1)}) fusion(pred[4,512]{1,0:T(4,128)(4,1)S(1)} %iota_compare_fusion.5, bf16[4,2,128,576]{2,3,1,0:T(8,128)(2,1)S(1)} %copy-done, bf16[4,512,576]{1,2,0:T(8,128)(2,1)} %param.8), kind=kOutput, calls=%fused_computation.10 | convolution fusion | flops 605551616 | bytes 5642240 | tf_op jit(solution)/shard_map/bqhw,blw->bqhl/dot_general | solution.py:20
  19.6 9.6 %all-to-all-done = bf16[16,16,640]{2,1,0:T(8,128)(2,1)} async-done(((bf16[16,16,640]{2,1,0:T(8,128)(2,1)}), bf16[16,16,640]{2,1,0:T(8,128)(2,1)}, u32[]{:S(2)}, u32[]{:S(2)}) %all-to-all-start) | async-done | bytes 327712 | tf_op jit(solution)/shard_map/all_to_all | solution.py:53
  29.2 1.0 fusion.28
  30.2 1.6 %fusion.38 = (f32[4,2,128]{2,1,0:T(2,128)S(1)}, f32[4,2,128,256]{2,3,1,0:T(8,128)S(1)}) fusion(bf16[4,2,128,576]{2,3,1,0:T(8,128)(2,1)S(1)} %copy-done, bf16[256,640]{1,0:T(8,128)(2,1)} %bitcast.9, pred[4,256]{1,0:T(4,128)(4,1)S(1)} %iota_compare_fusion.6), kind=kOutput, calls=%fused_computation.68 | convolution fusion | flops 302775296 | bytes 2561024 | tf_op jit(solution)/shard_map/bqhw,aw->bqha/dot_general | solution.py:21
  32.0 0.6 fusion.6
  32.6 0.8 copy-done.2
  33.5 1.1 %fusion.2 = f32[4,2,128,512]{3,2,1,0:T(8,128)S(1)} fusion(bf16[4,512,576]{1,2,0:T(8,128)(2,1)S(1)} %copy-done.2, f32[4,2,128,512]{3,2,1,0:T(8,128)S(1)} %get-tuple-element.6, f32[4,2,128]{2,1,0:T(2,128)S(1)} %add.60, f32[4,2,128]{2,1,0:T(2,128)S(1)} %max.8, pred[4,512]{1,0:T(4,128)(4,1)S(1)} %iota_compare_fusion.5), kind=kOutput, calls=%fused_computation.3 | convolution fusion | flops 539492352 | bytes 6301696 | tf_op jit(solution)/shard_map/bqhl,blc->bqhc/dot_general | solution.py:34
  34.6 1.4 %add_convert_fusion = bf16[4,2,128,512]{3,2,1,0:T(8,128)(2,1)S(1)} fusion(f32[4,2,128,512]{3,2,1,0:T(8,128)S(1)} %fusion.2, f32[4,2,128,256]{2,3,1,0:T(8,128)S(1)} %get-tuple-element.8, f32[4,2,128]{2,1,0:T(2,128)S(1)} %add.60, f32[4,2,128]{2,1,0:T(2,128)S(1)} %max.8, bf16[256,640]{1,0:T(8,128)(2,1)} %bitcast.9), kind=kOutput, calls=%fused_computation.5 | convolution fusion | flops 270270464 | bytes 4464640 | tf_op jit(solution)/shard_map/bqha,ac->bqhc/dot_general | solution.py:37
  36.0 2.1 %copy.24 = bf16[4,2,128,512]{3,1,0,2:T(2,128)(2,1)} copy(bf16[4,2,128,512]{3,2,1,0:T(8,128)(2,1)S(1)} %add_convert_fusion) | data formatting | bytes 2097152 | tf_op jit(solution)/shard_map/convert_element_type | solution.py:40
  38.1 10.7 %all-to-all-start.1 = ((bf16[4,2,128,512]{3,1,0,2:T(2,128)(2,1)}), bf16[4,2,128,512]{3,1,0,2:T(2,128)(2,1)S(1)}, u32[]{:S(2)}, u32[]{:S(2)}) async-start(bf16[4,2,128,512]{3,1,0,2:T(2,128)(2,1)} %copy.24), calls=%async_computation.1 | async-start | bytes 2097152 | tf_op jit(solution)/shard_map/all_to_all | solution.py:62
  48.9 0.6 reduce-window.6
  49.8 26.5 %all-to-all-done.1 = bf16[4,2,128,512]{3,1,0,2:T(2,128)(2,1)S(1)} async-done(((bf16[4,2,128,512]{3,1,0,2:T(2,128)(2,1)}), bf16[4,2,128,512]{3,1,0,2:T(2,128)(2,1)S(1)}, u32[]{:S(2)}, u32[]{:S(2)}) %all-to-all-start.1) | async-done | bytes 1048608 | tf_op jit(solution)/shard_map/all_to_all | solution.py:62
  76.2 0.4 copy.43
  77.0 1.5 %fusion.9 = bf16[128,2,4,128]{3,0,1,2:T(8,128)(2,1)S(1)} fusion(bf16[128,2,4,512]{3,0,1,2:T(8,128)(2,1)S(1)} %all_to_all.23, bf16[4,512,128]{2,1,0:T(8,128)(2,1)} %param.15), kind=kOutput, calls=%fused_computation.17 | convolution fusion | flops 134348800 | bytes 1835008 | tf_op jit(solution)/shard_map/bqhc,hcv->bqhv/dot_general | solution.py:60
  78.6 1.7 %scatter_custom_fusion = bf16[512,512]{1,0:T(8,128)(2,1)S(1)} fusion(s32[256]{0:T(256)S(1)} %bitcast.86, bf16[32,8,4,128]{3,2,1,0:T(4,128)(2,1)S(1)} %bitcast.80, bf16[]{:T(256)} %constant.10.clone.1), kind=kCustom, calls=%fused_computation.31 | custom fusion | bytes 786434 | tf_op jit(solution)/shard_map/scatter | solution.py:70
  80.3 21.2 %all_to_all.28 = bf16[16,32,512]{2,1,0:T(8,128)(2,1)S(1)} all-to-all(bf16[16,32,512]{2,1,0:T(8,128)(2,1)S(1)} %bitcast.78), channel_id=1, replica_groups=mesh['group'=16,'member'=32] {'group'}, dimensions={0} | all-to-all | bytes 1048576 | tf_op jit(solution)/shard_map/all_to_all | solution.py:71
  101.5 0.8 copy.45
  (23 shorter events, 1.3 us)
Async XLA Ops:
  0.0 16.8 %copy-start = (bf16[4,2,128,576]{2,3,1,0:T(8,128)(2,1)S(1)}, bf16[4,2,128,576]{2,3,1,0:T(8,128)(2,1)}, u32[]{:S(2)}) copy-start(bf16[4,2,128,576]{2,3,1,0:T(8,128)(2,1)} %param.10) | copy-start | bytes 3538948
  5.2 24.0 %all-to-all-start = ((bf16[16,16,640]{2,1,0:T(8,128)(2,1)}), bf16[16,16,640]{2,1,0:T(8,128)(2,1)}, u32[]{:S(2)}, u32[]{:S(2)}) async-start(bf16[16,16,640]{2,1,0:T(8,128)(2,1)} %bitcast.8), calls=%async_computation | async-start | bytes 655360 | tf_op jit(solution)/shard_map/all_to_all | solution.py:53
  31.8 1.7 %copy-start.2 = (bf16[4,512,576]{1,2,0:T(8,128)(2,1)S(1)}, bf16[4,512,576]{1,2,0:T(8,128)(2,1)}, u32[]{:S(2)}) copy-start(bf16[4,512,576]{1,2,0:T(8,128)(2,1)} %param.8) | copy-start | bytes 7077892
  36.0 12.8 %copy-start.1 = (s32[256,1]{0,1:T(1,128)S(1)}, s32[256,1]{0,1:T(1,128)}, u32[]{:S(2)}) copy-start(s32[256,1]{0,1:T(1,128)} %param.14) | copy-start | bytes 3076
  38.1 38.1 %all-to-all-start.1 = ((bf16[4,2,128,512]{3,1,0,2:T(2,128)(2,1)}), bf16[4,2,128,512]{3,1,0,2:T(2,128)(2,1)S(1)}, u32[]{:S(2)}, u32[]{:S(2)}) async-start(bf16[4,2,128,512]{3,1,0,2:T(2,128)(2,1)} %copy.24), calls=%async_computation.1 | async-start | bytes 2097152 | tf_op jit(solution)/shard_map/all_to_all | solution.py:62

commit v2 on v0

v2 whole, which is shorter than its diff:
```python
import functools

import jax
import jax.numpy as jnp
from jax import lax
from jax.experimental import pallas as pl
from jax.experimental.pallas import tpu as pltpu
from jax.sharding import PartitionSpec as P

KVL = 512
ROPE = 64
NOPE = 128
VH = 128
WIDTH = KVL + ROPE
WIDE = 640
SCALE = (NOPE + ROPE) ** (-0.5)
MESH = pl.DeviceIdType.MESH
F32 = jnp.float32
BF16 = jnp.bfloat16


def iota(shape, axis):
    return lax.broadcasted_iota(jnp.int32, shape, axis)


def swing(j, n):
    half = (j + 1) // 2
    return lax.rem(jnp.where(lax.rem(j, 2) == 1, half, n - half), n)


def group_peer(k, g, groups):
    rows = groups // 2
    y = lax.rem(g // 2 + swing(k // 2, rows), rows)
    return y * 2 + lax.rem(lax.rem(g, 2) + lax.rem(k, 2), 2)


def member_peer(k, m, members):
    rows = members // 4
    z = lax.rem(m // 4 + swing(k // 4, rows), rows)
    return z * 4 + lax.rem(lax.rem(m, 4) + lax.rem(k, 4), 4)


def one_hot_places(targets, peers, cap):
    n = targets.shape[1]
    named = iota((peers, n), 0) == targets
    earlier = (iota((n, n), 0) < iota((n, n), 1)).astype(BF16)
    counts = jnp.dot(named.astype(BF16), earlier, preferred_element_type=F32)
    slot = jnp.sum(jnp.where(named, counts, 0.0), 0, keepdims=True)
    where_to = targets * cap + slot.astype(jnp.int32)
    return (iota((peers * cap, n), 0) == where_to).astype(BF16)


def kernel(
    groups, members, lens_ref, dest_ref, slot_ref, tok_ref, fresh_ref, cache_hbm, query_hbm, w_hbm,
    out_ref,
    cache, query, weights, fresh_out, arrived, queries, top, total, near, bias, picks,
    lat_out, lat_in, disp,
    in_sem, fresh_ssem, fresh_rsem, lat_ssem, lat_rsem, disp_ssem, disp_rsem, own_sem,
):
    g, m = lax.axis_index("group"), lax.axis_index("member")
    count, keys = cache_hbm.shape[0], cache_hbm.shape[1]
    rows = query_hbm.shape[1]
    heads = w_hbm.shape[0]
    part = rows // heads
    qtok = part // members
    mine = count * qtok
    cap = fresh_out.shape[1]
    cape = disp.shape[1] // groups

    barrier = pltpu.get_barrier_semaphore()

    @pl.loop(1, groups)
    def _(k):
        pl.semaphore_signal(barrier, inc=1, device_id=(group_peer(k, g, groups), m), device_id_type=MESH)

    @pl.loop(1, members)
    def _(k):
        pl.semaphore_signal(barrier, inc=1, device_id=(g, member_peer(k, m, members)), device_id_type=MESH)

    def load_query(b):
        return pltpu.make_async_copy(query_hbm.at[b], query.at[b], in_sem.at[b])

    def load_cache(b):
        return pltpu.make_async_copy(cache_hbm.at[b], cache.at[b], in_sem.at[count + b])

    load_w = pltpu.make_async_copy(w_hbm, weights, in_sem.at[2 * count])
    for b in range(count):
        load_query(b).start()
        load_cache(b).start()
    load_w.start()

    places = one_hot_places(dest_ref[...], groups, cap)
    fresh_out[:, :, :WIDTH] = (
        jnp.dot(places, fresh_ref[...], preferred_element_type=F32)
        .astype(BF16)
        .reshape(groups, cap, WIDTH)
    )
    n = fresh_ref.shape[0]
    marks = (iota((128, n), 0) - 64 == slot_ref[...]).astype(BF16)
    marked = lax.dot_general(places, marks, (((1,), (1,)), ((), ())), preferred_element_type=F32)
    fresh_out[:, :, WIDTH:] = marked[:, 64:].astype(BF16).reshape(groups, cap, WIDE - WIDTH)

    pl.semaphore_wait(barrier, groups - 1 + members - 1)

    @pl.loop(1, groups)
    def _(k):
        e = group_peer(k, g, groups)
        pltpu.make_async_remote_copy(
            src_ref=fresh_out.at[e], dst_ref=arrived.at[g],
            send_sem=fresh_ssem.at[0], recv_sem=fresh_rsem.at[0],
            device_id=(e, m), device_id_type=MESH,
        ).start()

    arrived[g] = fresh_out[g]

    r, c = iota((rows, rows), 0), iota((rows, rows), 1)
    order = (lax.rem(r, qtok) * (rows // qtok) + lax.rem(r, part) // qtok * heads + r // part == c).astype(BF16)

    @pl.loop(0, count)
    def _(b):
        load_query(b).wait()
        load_cache(b).wait()
        q = jnp.dot(order, query[b], preferred_element_type=F32).astype(BF16)
        span = pl.ds(pl.multiple_of(b * part, part), part)
        queries[:, span, :] = q.reshape(heads, part, WIDTH)
        score = lax.dot_general(q, cache[b], (((1,), (1,)), ((), ())), preferred_element_type=F32) * SCALE
        score = jnp.where(iota((rows, keys), 1) < lens_ref[b], score, -jnp.inf)
        high = jnp.max(score, -1, keepdims=True)
        p = jnp.exp(score - high)
        top[:, span, :] = high.reshape(heads, part, 1)
        total[:, span, :] = jnp.sum(p, -1, keepdims=True).reshape(heads, part, 1)
        near[:, span, :] = jnp.dot(
            p.astype(BF16), cache[b, :, :KVL], preferred_element_type=F32
        ).reshape(heads, part, KVL)

    picks[...] = one_hot_places(tok_ref[...], groups, cape)
    load_w.wait()
    half = KVL // 2

    pltpu.make_async_copy(
        arrived.at[pl.ds(0, groups - 1)], arrived.at[pl.ds(0, groups - 1)], fresh_rsem.at[0]
    ).wait()
    pool = groups * cap
    chosen = (iota((8, 128), 1) - 64 == iota((8, 128), 0)).astype(BF16)
    labelled = lax.dot_general(
        chosen, arrived[:, :, KVL:].reshape(pool, WIDE - KVL), (((1,), (1,)), ((), ())),
        preferred_element_type=F32,
    )
    for b in range(count):
        bias[b * part : (b + 1) * part, :] = jnp.broadcast_to(
            jnp.where(labelled[b : b + 1, :] > 0.5, 0.0, -jnp.inf), (part, pool)
        )

    r, c = iota((rows, rows), 0), iota((rows, rows), 1)
    back = (lax.rem(r, mine) // qtok * part + r // mine * qtok + lax.rem(r, qtok) == c).astype(BF16)

    @pl.loop(0, heads)
    def _(h):
        keys_in = arrived[...].reshape(pool, WIDE)
        score = lax.dot_general(
            queries[h], keys_in[:, :WIDTH], (((1,), (1,)), ((), ())), preferred_element_type=F32
        )
        score = score * SCALE + bias[...]
        high = jnp.maximum(top[h], jnp.max(score, -1, keepdims=True))
        p = jnp.exp(score - high)
        shrink = jnp.exp(top[h] - high)
        norm = 1.0 / (total[h] * shrink + jnp.sum(p, -1, keepdims=True))
        far = jnp.dot(p.astype(BF16), keys_in[:, :KVL], preferred_element_type=F32)
        latent = ((near[h] * shrink + far) * norm).astype(BF16)
        moved = jnp.dot(back, latent, preferred_element_type=F32).reshape(members, mine, KVL)
        lat_out[h] = jnp.concatenate([moved[:, :, :half], moved[:, :, half:]], 1).astype(BF16)

        @pl.loop(1, members)
        def _(k):
            d = member_peer(k, m, members)
            pltpu.make_async_remote_copy(
                src_ref=lat_out.at[h, d], dst_ref=lat_in.at[h, m],
                send_sem=lat_ssem.at[h], recv_sem=lat_rsem.at[h],
                device_id=(g, d), device_id_type=MESH,
            ).start()

        lat_in[h, m] = lat_out[h, m]

    @pl.loop(0, heads)
    def _(h):
        pltpu.make_async_copy(
            lat_in.at[h, pl.ds(0, members - 1)], lat_in.at[h, pl.ds(0, members - 1)], lat_rsem.at[h]
        ).wait()
        w = jnp.concatenate([weights[h, :half, :], weights[h, half:, :]], 1)
        both = jnp.dot(
            lat_in[h].reshape(members * 2 * mine, half), w, preferred_element_type=F32
        ).reshape(members, 2 * mine, 2 * VH)
        value = (both[:, :mine, :VH] + both[:, mine:, VH:]).reshape(members * mine, VH).astype(BF16)
        disp[h] = jnp.dot(picks[...], value, preferred_element_type=F32).astype(BF16)
        columns = pl.ds(pl.multiple_of(h * VH, VH), VH)
        spot = out_ref.at[pl.ds(pl.multiple_of(g * cape, cape), cape), columns]

        @pl.loop(1, groups)
        def _(k):
            e = group_peer(k, g, groups)
            pltpu.make_async_remote_copy(
                src_ref=disp.at[h, pl.ds(pl.multiple_of(e * cape, cape), cape)], dst_ref=spot,
                send_sem=disp_ssem.at[h], recv_sem=disp_rsem.at[h],
                device_id=(e, m), device_id_type=MESH,
            ).start()

        pltpu.make_async_copy(
            disp.at[h, pl.ds(pl.multiple_of(g * cape, cape), cape)], spot, own_sem.at[h]
        ).start()

    def wait_for(ref, sem):
        pltpu.make_async_copy(ref, ref, sem).wait()

    wait_for(fresh_out.at[pl.ds(0, groups - 1)], fresh_ssem.at[0])

    @pl.loop(0, heads)
    def _(h):
        wait_for(lat_out.at[h, pl.ds(0, members - 1)], lat_ssem.at[h])
        wait_for(disp.at[h, pl.ds(0, (groups - 1) * cape)], disp_ssem.at[h])
        wait_for(disp.at[h, pl.ds(0, (groups - 1) * cape)], disp_rsem.at[h])
        wait_for(disp.at[h, pl.ds(0, cape)], own_sem.at[h])


def local(cache, cache_len, query, fresh, fresh_dest, fresh_slot, token_group, w_uv):
    groups, members = lax.axis_size("group"), lax.axis_size("member")
    count, qtok, all_heads = query.shape[:3]
    rows = qtok * all_heads
    heads = w_uv.shape[0]
    n = fresh.shape[0]
    cap = 2 * n // groups
    tokens = token_group.shape[0]
    cape = 2 * tokens // groups
    mine = count * qtok
    vmem = pl.BlockSpec(memory_space=pltpu.VMEM)
    anywhere = pl.BlockSpec(memory_space=pl.ANY)
    dma = pltpu.SemaphoreType.DMA
    return pl.pallas_call(
        functools.partial(kernel, groups, members),
        out_shape=jax.ShapeDtypeStruct((groups * cape, heads * VH), BF16),
        in_specs=[pl.BlockSpec(memory_space=pltpu.SMEM), vmem, vmem, vmem, vmem, anywhere, anywhere, anywhere],
        out_specs=anywhere,
        scratch_shapes=[
            pltpu.VMEM(cache.shape, BF16),
            pltpu.VMEM((count, rows, WIDTH), BF16),
            pltpu.VMEM(w_uv.shape, BF16),
            pltpu.VMEM((groups, cap, WIDE), BF16),
            pltpu.VMEM((groups, cap, WIDE), BF16),
            pltpu.VMEM((heads, rows * count // heads, WIDTH), BF16),
            pltpu.VMEM((heads, rows * count // heads, 1), F32),
            pltpu.VMEM((heads, rows * count // heads, 1), F32),
            pltpu.VMEM((heads, rows * count // heads, KVL), F32),
            pltpu.VMEM((rows * count // heads, groups * cap), F32),
            pltpu.VMEM((groups * cape, tokens), BF16),
            pltpu.VMEM((heads, members, 2 * mine, KVL // 2), BF16),
            pltpu.VMEM((heads, members, 2 * mine, KVL // 2), BF16),
            pltpu.VMEM((heads, groups * cape, VH), BF16),
            dma((2 * count + 1,)),
            dma((1,)),
            dma((1,)),
            dma((heads,)),
            dma((heads,)),
            dma((heads,)),
            dma((heads,)),
            dma((heads,)),
        ],
        compiler_params=pltpu.CompilerParams(
            collective_id=0, has_side_effects=True, vmem_limit_bytes=48 * 1024 * 1024
        ),
        cost_estimate=pl.CostEstimate(flops=2_500_000_000, bytes_accessed=6_000_000, transcendentals=800_000),
    )(
        cache_len,
        fresh_dest.reshape(1, n),
        fresh_slot.reshape(1, n),
        token_group.reshape(1, tokens),
        fresh,
        cache,
        query.reshape(count, rows, WIDTH),
        w_uv,
    )


def solution(mesh):
    placed = (
        P(("group", "member"), None, None),
        P(("group", "member")),
        P(("group", "member"), None, None, None),
        P(("group", "member"), None),
        P(("group", "member"), None),
        P(("group", "member")),
        P("group", None),
        P("member", None, None),
    )
    return jax.shard_map(
        local, mesh=mesh, in_specs=placed, out_specs=P("group", "member"), check_vma=False
    )
```

time: 147 us -> 69.6 us (0.47)
  Pallas kernels: 0 us -> 60.5 us
  waiting for transfers between devices: 54 us -> 0 us
  blocking collectives: 44.6 us -> 0 us
  matrix products: 13.5 us -> 0 us
  between operations: 13.5 us -> 0.08 us
  starting transfers between devices: 10.1 us -> 0 us
  other arithmetic: 4.71 us -> 0 us
  local copies, waits for them, and re-layouts: 6.19 us -> 8.72 us
    pallas_call x0 -> x1, Pallas kernels: none -> 60.5 us  [local(): pl.pallas_call(functools.partial(kernel, groups, members), out_shape=jax....]
    all_gather x1 -> x0, waiting for transfers between devices: 27.5 us -> none  [local(): lax.all_gather(fresh, 'group', axis=0, tiled=True)]
    all_to_all x1 -> x0, waiting for transfers between devices: 25.8 us -> none  [local(): lax.all_to_all(latent, 'member', split_axis=2, concat_axis=0, tiled=True)]
    all_to_all x1 -> x0, blocking collectives: 23.9 us -> none  [local(): lax.all_to_all(packed.reshape(groups, cape, values.shape[1]), 'group', sp...]
    all_gather x1 -> x0, blocking collectives: 20.7 us -> none  [local(): lax.all_gather(codes, 'group', axis=0, tiled=True)]
    dot_general x5 -> x0, matrix products: 13.5 us -> none  [the longest x1 5.58 us: attend(): jnp.einsum('bqhw,aw->bqha', query, arrived, preferred_element_type=jnp.fl...]
    all_to_all x1 -> x0, starting transfers between devices: 10.1 us -> none  [local(): lax.all_to_all(latent, 'member', split_axis=2, concat_axis=0, tiled=True)]
    unnamed x9 -> x16, local copies, waits for them, and re-layouts: 1.37 us -> 8.72 us
  transfers between devices with their start and end apart: 2 -> 0, of which waited for: 2 -> 0; matrix products, arithmetic and copies ran while one was open for 4% -> 0% of each run, Pallas kernels for 0% -> 0%
where the time goes in v2:
time: 69.6 us; the launch traced here: 69.3 us
  Pallas kernels  60.5 us (87%)
  local copies, waits for them, and re-layouts  8.72 us (13%)
    pallas_call x1, Pallas kernels, local(): pl.pallas_call(functools.partial(kernel, groups, members), out_shape=jax....  60.5 us
    unnamed x16, local copies, waits for them, and re-layouts  8.72 us

profile of v2, /device:TPU:1, one launch (start us, length us, event | category | flops | bytes accessed | tf_op | source)
XLA Modules:
  0.0 69.3 jit_solution(9579960832004277548)
XLA Ops:
  0.0 1.1 %copy.10.fresh_ref = bf16[128,576]{1,0:T(8,128)(2,1)S(1)} copy(bf16[128,576]{0,1:T(8,128)(2,1)} %param.11) | data formatting | bytes 294912 | tf_op args[3]
  1.1 2.4 %copy.9 = bf16[4,2,128,576]{3,2,1,0:T(8,128)(2,1)} copy(bf16[4,2,128,576]{2,3,1,0:T(8,128)(2,1)} %param.10) | data formatting | bytes 2359296 | tf_op args[2]
  3.5 0.0 copy-start.1
  3.5 0.0 copy-start.2
  3.5 0.0 copy-start.3
  3.5 0.0 copy-start.4
  3.5 0.0 copy-start.5
  3.5 3.1 %copy.11.cache_hbm = bf16[4,512,576]{2,1,0:T(8,128)(2,1)S(1)} copy(bf16[4,512,576]{1,2,0:T(8,128)(2,1)} %param.8) | data formatting | bytes 4718592 | tf_op args[0]
  6.6 0.0 copy-done.1
  6.6 0.0 copy-done.2
  6.7 0.0 copy-done.3
  6.7 0.0 copy-done.4
  6.7 0.0 copy-done.5
  6.7 0.0 copy-start
  6.7 1.3 %copy-done = bf16[4,2,128,576]{3,2,1,0:T(8,128)(2,1)S(1)} copy-done((bf16[4,2,128,576]{3,2,1,0:T(8,128)(2,1)S(1)}, bf16[4,2,128,576]{3,2,1,0:T(8,128)(2,1)}, u32[]{:S(2)}) %copy-start) | copy-done | bytes 1179672
  8.0 60.5 %shard_map.82 = bf16[512,512]{1,0:T(8,128)(2,1)S(1)} custom-call(s32[4]{0:T(128)S(1)} %copy-done.3, s32[1,128]{1,0:T(1,128)S(1)} %bitcast.6, s32[1,128]{1,0:T(1,128)S(1)} %bitcast.7, s32[1,256]{1,0:T(1,128)S(1)} %bitcast.5, bf16[128,576]{1,0:T(8,128)(2,1)S(1)} %copy.10.fresh_ref, bf16[4,512,576]{2,1,0:T(8,128)(2,1)S(1)} %copy.11.cache_hbm, ...), custom_call_target="tpu_custom_call" | custom-call | flops 2500000000 | bytes 6000000 | tf_op jit(solution)/shard_map/pallas_call | solution.py:237
  68.5 0.8 %copy.13 = bf16[512,512]{1,0:T(8,128)(2,1)} copy(bf16[512,512]{1,0:T(8,128)(2,1)S(1)} %shard_map.82) | data formatting | bytes 1048576
Async XLA Ops:
  3.5 3.2 %copy-start.1 = (bf16[4,512,128]{2,1,0:T(8,128)(2,1)S(1)}, bf16[4,512,128]{2,1,0:T(8,128)(2,1)}, u32[]{:S(2)}) copy-start(bf16[4,512,128]{2,1,0:T(8,128)(2,1)} %w_hbm.1) | copy-start | bytes 1572868
  3.5 3.2 %copy-start.2 = (s32[256,1]{0,1:T(1,128)S(1)}, s32[256,1]{0,1:T(1,128)}, u32[]{:S(2)}) copy-start(s32[256,1]{0,1:T(1,128)} %param.14) | copy-start | bytes 3076
  3.5 3.2 %copy-start.3 = (s32[4]{0:T(128)S(1)}, s32[4]{0:T(128)}, u32[]{:S(2)}) copy-start(s32[4]{0:T(128)} %lens_ref.1) | copy-start | bytes 52
  3.5 3.2 %copy-start.4 = (s32[128,1]{0,1:T(1,128)S(1)}, s32[128,1]{0,1:T(1,128)}, u32[]{:S(2)}) copy-start(s32[128,1]{0,1:T(1,128)} %param.12) | copy-start | bytes 1540
  3.5 3.2 %copy-start.5 = (s32[128]{0:T(128)S(1)}, s32[128]{0:T(128)}, u32[]{:S(2)}) copy-start(s32[128]{0:T(128)} %param.13) | copy-start | bytes 1540
  6.7 1.3 %copy-start = (bf16[4,2,128,576]{3,2,1,0:T(8,128)(2,1)S(1)}, bf16[4,2,128,576]{3,2,1,0:T(8,128)(2,1)}, u32[]{:S(2)}) copy-start(bf16[4,2,128,576]{3,2,1,0:T(8,128)(2,1)} %copy.9) | copy-start | bytes 3538948

commit v3 on v2

v3 whole, which is shorter than its diff:
```python
import functools

import jax
import jax.numpy as jnp
from jax import lax
from jax.experimental import pallas as pl
from jax.experimental.pallas import tpu as pltpu
from jax.sharding import PartitionSpec as P

KVL = 512
ROPE = 64
NOPE = 128
VH = 128
WIDTH = KVL + ROPE
WIDE = 640
SCALE = (NOPE + ROPE) ** (-0.5)
MESH = pl.DeviceIdType.MESH
F32 = jnp.float32
BF16 = jnp.bfloat16
REACH = 2
NT = (((1,), (1,)), ((), ()))


def iota(shape, axis):
    return lax.broadcasted_iota(jnp.int32, shape, axis)


def swing(j):
    return ((j + 1) >> 1) * (2 * (j & 1) - 1)


def group_peer(k, g, groups):
    return ((((g >> 1) + swing(k >> 1)) & (groups // 2 - 1)) << 1) | ((g ^ k) & 1)


def one_hot_places(targets, peers, cap):
    n = targets.shape[1]
    named = iota((peers, n), 0) == targets
    earlier = (iota((n, n), 0) < iota((n, n), 1)).astype(BF16)
    counts = jnp.dot(named.astype(BF16), earlier, preferred_element_type=F32)
    slot = jnp.sum(jnp.where(named, counts, 0.0), 0, keepdims=True)
    where_to = targets * cap + slot.astype(jnp.int32)
    return (iota((peers * cap, n), 0) == where_to).astype(BF16)


def kernel(
    groups, members, lens_hbm, dest_hbm, slot_hbm, tok_hbm, fresh_hbm, cache_hbm, query_hbm, w_hbm,
    out_ref,
    lens, dest, slot, tok, fresh, cache, query, weights, fresh_out, arrived, queries, top, total, near,
    bias, picks, back, lat_out, lat_in, val_out, val_in, disp,
    in_sem, fresh_ssem, fresh_rsem, ring_ssem, ring_rsem, twin_ssem, twin_rsem,
    lat_ssem, lat_rsem, side_ssem, side_rsem, val_ssem, val_rsem, disp_ssem, disp_rsem, own_sem,
):
    g, m = lax.axis_index("group"), lax.axis_index("member")
    count, keys = cache_hbm.shape[0], cache_hbm.shape[2]
    qtok = query_hbm.shape[1]
    rows = qtok * query_hbm.shape[3]
    heads = w_hbm.shape[0]
    part = rows // heads
    mine = count * qtok
    cap = fresh_out.shape[1]
    cape = disp.shape[1] // groups
    nx = 4
    nz = members // nx
    z, x, core = m >> 2, m & 3, g & 1
    half = KVL // 2
    pair = heads // 2

    def at_z(k):
        return (((z + k) & (nz - 1)) << 2) | x

    def at_x(k):
        return (z << 2) | ((x + k) & 3)

    def load(src, dst, i):
        return pltpu.make_async_copy(src, dst, in_sem.at[i])

    small = [
        load(fresh_hbm, fresh, 0), load(dest_hbm, dest, 1), load(slot_hbm, slot, 2),
        load(tok_hbm, tok, 3), load(lens_hbm, lens, 4),
    ]
    load_w = load(w_hbm, weights.at[REACH], 5)
    queries_in = [load(query_hbm.at[b], query.at[b], 6 + b) for b in range(count)]
    cache_in = [load(cache_hbm.at[b], cache.at[b], 6 + count + b) for b in range(count)]
    for copy in small:
        copy.start()

    barrier = pltpu.get_barrier_semaphore()

    @pl.loop(1, groups)
    def _(k):
        pl.semaphore_signal(barrier, inc=1, device_id=(group_peer(k, g, groups), m), device_id_type=MESH)

    @pl.loop(1, nz)
    def _(k):
        pl.semaphore_signal(barrier, inc=1, device_id=(g, at_z(k)), device_id_type=MESH)

    @pl.loop(1, nx)
    def _(k):
        pl.semaphore_signal(barrier, inc=1, device_id=(g, at_x(k)), device_id_type=MESH)
        for step in (-2, -1, 1, 2):
            aside = (at_z(step) & ~3) | ((x + k) & 3)
            pl.semaphore_signal(barrier, inc=1, device_id=(g, aside), device_id_type=MESH)

    load_w.start()
    for b in range(count):
        queries_in[b].start()
        cache_in[b].start()
    for copy in small:
        copy.wait()

    places = one_hot_places(dest[...], groups, cap)
    fresh_out[:, :, :WIDTH] = (
        lax.dot_general(places, fresh[...], NT, preferred_element_type=F32)
        .astype(BF16)
        .reshape(groups, cap, WIDTH)
    )
    n = fresh.shape[1]
    marks = (iota((128, n), 0) - 64 == slot[...]).astype(BF16)
    marked = lax.dot_general(places, marks, NT, preferred_element_type=F32)
    fresh_out[:, :, WIDTH:] = marked[:, 64:].astype(BF16).reshape(groups, cap, WIDE - WIDTH)

    pl.semaphore_wait(barrier, groups - 1 + nz - 1 + 5 * (nx - 1))

    @pl.loop(1, groups)
    def _(k):
        e = group_peer(groups - k, g, groups)
        pltpu.make_async_remote_copy(
            src_ref=fresh_out.at[e], dst_ref=arrived.at[g],
            send_sem=fresh_ssem.at[0], recv_sem=fresh_rsem.at[0],
            device_id=(e, m), device_id_type=MESH,
        ).start()

    arrived[g] = fresh_out[g]

    def piece(k, ab, side):
        return weights.at[
            REACH + k, pl.ds(ab * pair, pair), pl.ds(pl.multiple_of(side * half, half), half)
        ]

    def ring_copy(step, way, ab):
        sign = 1 - 2 * way
        return pltpu.make_async_remote_copy(
            src_ref=piece(-sign * (step - 1), ab, core), dst_ref=piece(-sign * step, ab, core),
            send_sem=ring_ssem.at[step - 1, way, ab], recv_sem=ring_rsem.at[step - 1, way, ab],
            device_id=(g, at_z(sign)), device_id_type=MESH,
        )

    def twin_copy(step, way, ab):
        sign = 1 - 2 * way
        return pltpu.make_async_remote_copy(
            src_ref=piece(-sign * step, ab, core), dst_ref=piece(-sign * step, ab, core),
            send_sem=twin_ssem.at[step - 1, way, ab], recv_sem=twin_rsem.at[step - 1, way, ab],
            device_id=(g ^ 1, m), device_id_type=MESH,
        )

    def wait_for(ref, sem):
        pltpu.make_async_copy(ref, ref, sem).wait()

    def ring_pass(step, ab):
        for way in range(2):
            here = piece(-(1 - 2 * way) * step, ab, core)
            wait_for(here, ring_rsem.at[step - 1, way, ab])
            if step < REACH:
                ring_copy(step + 1, way, ab).start()
            twin_copy(step, way, ab).start()

    def twin_wait(ab):
        for step in range(1, REACH + 1):
            for way in range(2):
                there = piece(-(1 - 2 * way) * step, ab, 1 - core)
                wait_for(there, twin_rsem.at[step - 1, way, ab])

    load_w.wait()
    for ab in range(2):
        for way in range(2):
            ring_copy(1, way, ab).start()

    r, c = iota((rows, rows), 0), iota((rows, rows), 1)
    order = (lax.rem(r, qtok) * (rows // qtok) + lax.rem(r, part) // qtok * heads + r // part == c).astype(BF16)
    for b in range(count):
        queries_in[b].wait()
        cache_in[b].wait()
        columns = jnp.concatenate([query[b, i] for i in range(qtok)], 1)
        q = lax.dot_general(order, columns, NT, preferred_element_type=F32).astype(BF16)
        span = pl.ds(b * part, part)
        queries[:, span, :] = q.reshape(heads, part, WIDTH)
        score = jnp.dot(q, cache[b], preferred_element_type=F32) * SCALE
        score = jnp.where(iota((rows, keys), 1) < lens[b], score, -jnp.inf)
        high = jnp.max(score, -1, keepdims=True)
        p = jnp.exp(score - high)
        top[:, span, :] = high.reshape(heads, part, 1)
        total[:, span, :] = jnp.sum(p, -1, keepdims=True).reshape(heads, part, 1)
        near[:, span, :] = lax.dot_general(
            p.astype(BF16), cache[b, :KVL, :], NT, preferred_element_type=F32
        ).reshape(heads, part, KVL)

    picks[...] = one_hot_places(tok[...], groups, cape)
    r, c = iota((rows, rows), 0), iota((rows, rows), 1)
    whose = ((r // mine + z + nz // 2) & (nz - 1)) * nx + r // (mine * nz)
    back[...] = (lax.rem(r, mine) // qtok * part + whose * qtok + lax.rem(r, qtok) == c).astype(BF16)

    for ab in range(2):
        ring_pass(1, ab)

    wait_for(arrived.at[pl.ds(0, groups - 1)], fresh_rsem.at[0])
    pool = groups * cap
    chosen = (iota((8, 128), 1) - 64 == iota((8, 128), 0)).astype(BF16)
    labelled = lax.dot_general(
        chosen, arrived[:, :, KVL:].reshape(pool, WIDE - KVL), NT,
        preferred_element_type=F32,
    )
    for b in range(count):
        bias[b * part : (b + 1) * part, :] = jnp.broadcast_to(
            jnp.where(labelled[b : b + 1, :] > 0.5, 0.0, -jnp.inf), (part, pool)
        )

    def attend(h):
        keys_in = arrived[...].reshape(pool, WIDE)
        score = lax.dot_general(queries[h], keys_in[:, :WIDTH], NT, preferred_element_type=F32)
        score = score * SCALE + bias[...]
        high = jnp.maximum(top[h], jnp.max(score, -1, keepdims=True))
        p = jnp.exp(score - high)
        shrink = jnp.exp(top[h] - high)
        norm = 1.0 / (total[h] * shrink + jnp.sum(p, -1, keepdims=True))
        far = jnp.dot(p.astype(BF16), keys_in[:, :KVL], preferred_element_type=F32)
        latent = ((near[h] * shrink + far) * norm).astype(BF16)
        moved = jnp.dot(back[...], latent, preferred_element_type=F32).reshape(nx, nz, mine, KVL)
        lat_out[h] = jnp.concatenate([moved[..., :half], moved[..., half:]], 2).astype(BF16)

    near_slots = 2 * REACH + 1

    def far_way(h):
        return 1 - 2 * (h & 1)

    def send_latents(h):
        @pl.loop(0, nx)
        def _(k):
            to = (x + k) & 3
            for source, slot, step in ((0, 7, 2 * far_way(h)), (7, 5, 1), (1, 6, -1)):
                pltpu.make_async_remote_copy(
                    src_ref=lat_out.at[h, to, source], dst_ref=lat_in.at[h, x, slot],
                    send_sem=side_ssem.at[h], recv_sem=side_rsem.at[h],
                    device_id=(g, (((z + step) & (nz - 1)) << 2) | to), device_id_type=MESH,
                ).start()

        for k in (2, 1, 3):
            pltpu.make_async_remote_copy(
                src_ref=lat_out.at[h, (x + k) & 3, pl.ds(2, near_slots)],
                dst_ref=lat_in.at[h, x, pl.ds(0, near_slots)],
                send_sem=lat_ssem.at[h], recv_sem=lat_rsem.at[h],
                device_id=(g, at_x(k)), device_id_type=MESH,
            ).start()

        lat_in[h, x, :near_slots] = lat_out[h, x, 2 : 2 + near_slots]

    def project(h):
        wait_for(lat_in.at[h, pl.ds(0, nx - 1), pl.ds(0, near_slots)], lat_rsem.at[h])
        wait_for(lat_in.at[h, pl.ds(0, nx), pl.ds(0, 3)], side_rsem.at[h])
        way = far_way(h)
        plan = [(k, 0) for k in range(-REACH, REACH + 1)] + [(2, -1), (-2, 1), (2 * way, -2 * way)]
        for k in (REACH, -REACH, 1, -1, 0):
            slots = [i for i, (owner, _) in enumerate(plan) if owner == k]
            w = jnp.concatenate([weights[REACH + k, h, :half, :], weights[REACH + k, h, half:, :]], 1)
            taken = [lat_in[h, :, i].reshape(nx * 2 * mine, half) for i in slots]
            both = jnp.dot(
                jnp.concatenate(taken, 0), w, preferred_element_type=F32
            ).reshape(len(slots), nx, 2 * mine, 2 * VH)
            value = both[:, :, :mine, :VH] + both[:, :, mine:, VH:]
            for j, i in enumerate(slots):
                block = value[j].reshape(nx * mine, VH).astype(BF16)
                if k == 0:
                    val_in[h, z] = block
                    continue
                val_out[h, i] = block
                pltpu.make_async_remote_copy(
                    src_ref=val_out.at[h, i], dst_ref=val_in.at[h, (z + plan[i][1]) & (nz - 1)],
                    send_sem=val_ssem.at[h], recv_sem=val_rsem.at[h],
                    device_id=(g, at_z(k)), device_id_type=MESH,
                ).start()

    def dispatch(h):
        wait_for(val_in.at[h, pl.ds(0, nz - 1)], val_rsem.at[h])
        value = val_in[h].reshape(members * mine, VH)
        disp[h] = jnp.dot(picks[...], value, preferred_element_type=F32).astype(BF16)
        spot = out_ref.at[pl.ds(pl.multiple_of(g * cape, cape), cape), pl.ds(h * VH, VH)]

        @pl.loop(1, groups)
        def _(k):
            e = group_peer(groups - k, g, groups)
            pltpu.make_async_remote_copy(
                src_ref=disp.at[h, pl.ds(pl.multiple_of(e * cape, cape), cape)], dst_ref=spot,
                send_sem=disp_ssem.at[h], recv_sem=disp_rsem.at[h],
                device_id=(e, m), device_id_type=MESH,
            ).start()

        pltpu.make_async_copy(
            disp.at[h, pl.ds(pl.multiple_of(g * cape, cape), cape)], spot, own_sem.at[h]
        ).start()

    attend(0)
    send_latents(0)
    ring_pass(2, 0)
    attend(1)
    send_latents(1)
    ring_pass(2, 1)
    attend(2)
    send_latents(2)
    twin_wait(0)
    project(0)
    attend(3)
    send_latents(3)
    project(1)
    dispatch(0)
    twin_wait(1)
    project(2)
    dispatch(1)
    project(3)
    dispatch(2)
    dispatch(3)

    wait_for(fresh_out.at[pl.ds(0, groups - 1)], fresh_ssem.at[0])
    for step in range(1, REACH + 1):
        for way in range(2):
            for ab in range(2):
                wait_for(piece(0, ab, core), ring_ssem.at[step - 1, way, ab])
                wait_for(piece(0, ab, core), twin_ssem.at[step - 1, way, ab])

    @pl.loop(0, heads)
    def _(h):
        wait_for(lat_out.at[h, pl.ds(0, nx - 1), pl.ds(0, near_slots)], lat_ssem.at[h])
        wait_for(lat_out.at[h, pl.ds(0, nx), pl.ds(0, 3)], side_ssem.at[h])
        wait_for(val_out.at[h, pl.ds(0, nz - 1)], val_ssem.at[h])
        wait_for(disp.at[h, pl.ds(0, (groups - 1) * cape)], disp_ssem.at[h])
        wait_for(disp.at[h, pl.ds(0, (groups - 1) * cape)], disp_rsem.at[h])
        wait_for(disp.at[h, pl.ds(0, cape)], own_sem.at[h])


def local(cache, cache_len, query, fresh, fresh_dest, fresh_slot, token_group, w_uv):
    groups, members = lax.axis_size("group"), lax.axis_size("member")
    count, qtok, all_heads = query.shape[:3]
    rows = qtok * all_heads
    heads = w_uv.shape[0]
    n = fresh.shape[0]
    cap = 2 * n // groups
    tokens = token_group.shape[0]
    cape = 2 * tokens // groups
    mine = count * qtok
    block = rows * count // heads
    nx = 4
    nz = members // nx
    anywhere = pl.BlockSpec(memory_space=pl.ANY)
    dma = pltpu.SemaphoreType.DMA
    return pl.pallas_call(
        functools.partial(kernel, groups, members),
        out_shape=jax.ShapeDtypeStruct((groups * cape, heads * VH), BF16),
        in_specs=[anywhere] * 8,
        out_specs=anywhere,
        scratch_shapes=[
            pltpu.SMEM((count,), jnp.int32),
            pltpu.VMEM((1, n), jnp.int32),
            pltpu.VMEM((1, n), jnp.int32),
            pltpu.VMEM((1, tokens), jnp.int32),
            pltpu.VMEM((WIDTH, n), BF16),
            pltpu.VMEM((count, WIDTH, cache.shape[1]), BF16),
            pltpu.VMEM((count, qtok, WIDTH, all_heads), BF16),
            pltpu.VMEM((2 * REACH + 1,) + w_uv.shape, BF16),
            pltpu.VMEM((groups, cap, WIDE), BF16),
            pltpu.VMEM((groups, cap, WIDE), BF16),
            pltpu.VMEM((heads, block, WIDTH), BF16),
            pltpu.VMEM((heads, block, 1), F32),
            pltpu.VMEM((heads, block, 1), F32),
            pltpu.VMEM((heads, block, KVL), F32),
            pltpu.VMEM((block, groups * cap), F32),
            pltpu.VMEM((groups * cape, tokens), BF16),
            pltpu.VMEM((rows, rows), BF16),
            pltpu.VMEM((heads, nx, nz, 2 * mine, KVL // 2), BF16),
            pltpu.VMEM((heads, nx, nz, 2 * mine, KVL // 2), BF16),
            pltpu.VMEM((heads, nz, nx * mine, VH), BF16),
            pltpu.VMEM((heads, nz, nx * mine, VH), BF16),
            pltpu.VMEM((heads, groups * cape, VH), BF16),
            dma((6 + 2 * count,)),
            dma((1,)),
            dma((1,)),
            dma((REACH, 2, 2)),
            dma((REACH, 2, 2)),
            dma((REACH, 2, 2)),
            dma((REACH, 2, 2)),
            dma((heads,)),
            dma((heads,)),
            dma((heads,)),
            dma((heads,)),
            dma((heads,)),
            dma((heads,)),
            dma((heads,)),
            dma((heads,)),
            dma((heads,)),
        ],
        compiler_params=pltpu.CompilerParams(
            collective_id=0, has_side_effects=True, vmem_limit_bytes=60 * 1024 * 1024
        ),
        cost_estimate=pl.CostEstimate(flops=2_500_000_000, bytes_accessed=6_000_000, transcendentals=800_000),
    )(
        cache_len,
        fresh_dest.reshape(1, n),
        fresh_slot.reshape(1, n),
        token_group.reshape(1, tokens),
        fresh.T,
        cache.transpose(0, 2, 1),
        query.transpose(0, 1, 3, 2),
        w_uv,
    )


def solution(mesh):
    placed = (
        P(("group", "member"), None, None),
        P(("group", "member")),
        P(("group", "member"), None, None, None),
        P(("group", "member"), None),
        P(("group", "member"), None),
        P(("group", "member")),
        P("group", None),
        P("member", None, None),
    )
    return jax.shard_map(
        local, mesh=mesh, in_specs=placed, out_specs=P("group", "member"), check_vma=False
    )
```

time: 69.6 us -> 54 us (0.78)
  Pallas kernels: 60.5 us -> 51.9 us
  local copies, waits for them, and re-layouts: 8.72 us -> 1.87 us
    pallas_call x1, Pallas kernels: 60.5 us -> 51.9 us  [local(): pl.pallas_call(functools.partial(kernel, groups, members), out_shape=jax....]
    unnamed x16 -> x1, local copies, waits for them, and re-layouts: 8.72 us -> 1.87 us
where the time goes in v3:
time: 54 us; the launch traced here: 53.8 us
  Pallas kernels  51.9 us (96%)
  local copies, waits for them, and re-layouts  1.87 us (3%)
    pallas_call x1, Pallas kernels, local(): pl.pallas_call(functools.partial(kernel, groups, members), out_shape=jax....  51.9 us
    unnamed x1, local copies, waits for them, and re-layouts  1.87 us

profile of v3, /device:TPU:1, one launch (start us, length us, event | category | flops | bytes accessed | tf_op | source)
XLA Modules:
  0.0 53.8 jit_solution(2632450056545279419)
XLA Ops:
  0.0 51.9 %shard_map.82 = bf16[512,512]{1,0:T(8,128)(2,1)} custom-call(s32[4]{0:T(128)} %lens_hbm.1, s32[1,128]{1,0:T(1,128)} %bitcast.10, s32[1,128]{1,0:T(1,128)} %bitcast.11, s32[1,256]{1,0:T(1,128)} %bitcast.9, bf16[576,128]{1,0:T(8,128)(2,1)} %bitcast.8, bf16[4,576,512]{2,1,0:T(8,128)(2,1)} %bitcast.6, bf16[4,2,576,128]{3,2,1,0:T(8,128)(2,1)} %bitcast.7, ...), custom_call_target="tpu_custom_call" | custom-call | flops 2500000000 | bytes 6000000 | tf_op jit(solution)/shard_map/pallas_call | solution.py:354
  52.0 1.9 %copy.10 = bf16[512,512]{1,0:T(8,128)(2,1)} copy(bf16[512,512]{1,0:T(8,128)(2,1)} %shard_map.82) | data formatting | bytes 1048576

commit v4 on v3

--- a/solution.py
+++ b/solution.py
@@ -82,14 +82,11 @@
     load_w = load(w_hbm, weights.at[REACH], 5)
     queries_in = [load(query_hbm.at[b], query.at[b], 6 + b) for b in range(count)]
     cache_in = [load(cache_hbm.at[b], cache.at[b], 6 + count + b) for b in range(count)]
-    for copy in small:
-        copy.start()
-
     barrier = pltpu.get_barrier_semaphore()
 
     @pl.loop(1, groups)
     def _(k):
-        pl.semaphore_signal(barrier, inc=1, device_id=(group_peer(k, g, groups), m), device_id_type=MESH)
+        pl.semaphore_signal(barrier, inc=1, device_id=(group_peer(groups - k, g, groups), m), device_id_type=MESH)
 
     @pl.loop(1, nz)
     def _(k):
@@ -102,6 +99,8 @@
             aside = (at_z(step) & ~3) | ((x + k) & 3)
             pl.semaphore_signal(barrier, inc=1, device_id=(g, aside), device_id_type=MESH)
 
+    for copy in small:
+        copy.start()
     load_w.start()
     for b in range(count):
         queries_in[b].start()
@@ -124,7 +123,7 @@
 
     @pl.loop(1, groups)
     def _(k):
-        e = group_peer(groups - k, g, groups)
+        e = group_peer(jnp.where(k <= groups // 2, groups + 1 - 2 * k, 2 * (groups - k)), g, groups)
         pltpu.make_async_remote_copy(
             src_ref=fresh_out.at[e], dst_ref=arrived.at[g],
             send_sem=fresh_ssem.at[0], recv_sem=fresh_rsem.at[0],
@@ -287,7 +286,7 @@
 
         @pl.loop(1, groups)
         def _(k):
-            e = group_peer(groups - k, g, groups)
+            e = group_peer(jnp.where(k <= groups // 2, groups + 1 - 2 * k, 2 * (groups - k)), g, groups)
             pltpu.make_async_remote_copy(
                 src_ref=disp.at[h, pl.ds(pl.multiple_of(e * cape, cape), cape)], dst_ref=spot,
                 send_sem=disp_ssem.at[h], recv_sem=disp_rsem.at[h],

time: 54 us -> 53.3 us (0.987)
  Pallas kernels: 51.9 us -> 51.2 us
    pallas_call x1, Pallas kernels: 51.9 us -> 51.2 us  [local(): pl.pallas_call(functools.partial(kernel, groups, members), out_shape=jax....]
where the time goes in v4:
time: 53.3 us; the launch traced here: 53.1 us
  Pallas kernels  51.2 us (96%)
  local copies, waits for them, and re-layouts  1.87 us (4%)
    pallas_call x1, Pallas kernels, local(): pl.pallas_call(functools.partial(kernel, groups, members), out_shape=jax....  51.2 us
    unnamed x1, local copies, waits for them, and re-layouts  1.87 us

profile of v4, /device:TPU:1, one launch (start us, length us, event | category | flops | bytes accessed | tf_op | source)
XLA Modules:
  0.0 53.1 jit_solution(13035121609046993822)
XLA Ops:
  0.0 51.2 %shard_map.82 = bf16[512,512]{1,0:T(8,128)(2,1)} custom-call(s32[4]{0:T(128)} %lens_hbm.1, s32[1,128]{1,0:T(1,128)} %bitcast.10, s32[1,128]{1,0:T(1,128)} %bitcast.11, s32[1,256]{1,0:T(1,128)} %bitcast.9, bf16[576,128]{1,0:T(8,128)(2,1)} %bitcast.8, bf16[4,576,512]{2,1,0:T(8,128)(2,1)} %bitcast.6, bf16[4,2,576,128]{3,2,1,0:T(8,128)(2,1)} %bitcast.7, ...), custom_call_target="tpu_custom_call" | custom-call | flops 2500000000 | bytes 6000000 | tf_op jit(solution)/shard_map/pallas_call | solution.py:353
  51.3 1.9 %copy.10 = bf16[512,512]{1,0:T(8,128)(2,1)} copy(bf16[512,512]{1,0:T(8,128)(2,1)} %shard_map.82) | data formatting | bytes 1048576
